TPU v7x, 256 devices: a whole 4x4x8 slice. The times are simulated.
256 devices in a mesh: blk: 8 (over x, y_hi), dom: 32 (over z, y_lo, core).
Axes of the slice: x: 4, y: 4 (y_hi: 2, y_lo: 2; y = y_hi * 2 + y_lo), z: 8, core: 2. Of those that a mesh axis runs over, the one named last changes fastest.
Arguments:
- orbitals: float32 [8, 256, 256, 256], P('blk', 'dom'), may hold values from -7 to 7
- dielectric: float32 [256, 256, 256], P('dom'), may hold values from 1 to 10
Outputs:
- exchange: float32 [8, 256, 256, 256], P('blk', 'dom')
All inputs are finite; a program needn't handle non-finite values.
Results may differ from a plain program's by a relative error of at most 0.0001.
Values sent between devices are 32-bit elements; how exact they have to be, the bound alone decides.
A program may use at most 128 MiB of HBM per device.

v0:
```python
import functools
import math

import jax
import jax.numpy as jnp
from jax import lax
from jax.experimental import pallas as pl
from jax.experimental.pallas import tpu as pltpu
from jax.sharding import PartitionSpec as P

FOUR_PI = 4.0 * math.pi
ITERS = 3
SCALE = 1.0 / 16.0
CHUNKS = 4
AHEAD = 2
SEQUENCE = (0, 3, 1, 2)
STRIP = 16
F32 = jnp.float32


def kernel(cx, cz, orb, eps, out, *scratch):
    (o, e, eblock, wx, wyp, wym, wzp, wzm, field, pack, rows, erows, red, zin, yred, yin, far_out, near_out, u_out, u_in,
     own_s, far_s, far_r, third_s, third_r, eps_s, plane_s, plane_r, row_s, row_r, z_s, z_r, y_s, y_r, near_s, out_s,
     out_r, u_s, u_r) = scratch
    planes, height, lanes = o.shape[1:]
    step = planes // CHUNKS
    blk, dom = lax.axis_index("blk"), lax.axis_index("dom")
    x, yh = blk // 2, blk % 2
    z, yl, core = dom // 4, (dom // 2) % 2, dom % 2
    dx = 1 - 2 * yh

    def flip(value, by):
        return value + by - 2 * by * value if by else value

    def device(x_, yh_, z_, yl_, core_):
        x_, z_ = lax.rem(x_ + cx, cx), lax.rem(z_ + cz, cz)
        return {"blk": x_ * 2 + yh_, "dom": z_ * 4 + yl_ * 2 + core_}

    def remote(src, dst, send, recv, to):
        return pltpu.make_async_remote_copy(src_ref=src, dst_ref=dst, send_sem=send, recv_sem=recv, device_id=to)

    def arrived(dst, recv):
        pltpu.make_async_copy(dst, dst, recv).wait()

    def sent(src, send):
        pltpu.make_async_copy(src, src, send).wait()

    barrier = pltpu.get_barrier_semaphore()
    partners = []
    for k in range(4):
        for cc in range(2):
            if k or cc:
                partners.append(device(x, flip(yh, k // 2), z, flip(yl, k % 2), flip(core, cc)))
    partners += [device(x + 1, yh, z, yl, core), device(x - 1, yh, z, yl, core)]
    partners += [device(x, yh, z + d, yl, core) for d in range(1, cz)]
    below, above = lax.rem(dom + 4 * cz - 1, 4 * cz), lax.rem(dom + 1, 4 * cz)
    to_plane = {"blk": blk, "dom": below}, {"blk": blk, "dom": above}
    partners += to_plane
    for k in range(2):
        for cc in range(2):
            partners.append(device(x + dx, 1 - yh, z, flip(yl, k), flip(core, cc)))
    for partner in partners:
        pl.semaphore_signal(barrier, inc=1, device_id=partner)
    pl.semaphore_wait(barrier, len(partners))

    across, aside, back = device(x, 1 - yh, z, yl, core), device(x + dx, yh, z, yl, core), device(x - dx, yh, z, yl, core)
    mine, theirs = pl.ds(height * yh, height), pl.ds(height * (1 - yh), height)

    def part(chunk):
        return pl.ds(chunk * step, step)

    def send(chunk):
        remote(orb.at[0, part(chunk), theirs], o.at[1, part(chunk)], far_s.at[chunk], far_r.at[chunk], across).start()
        remote(orb.at[0, part(chunk), mine], o.at[2, part(chunk)], third_s.at[chunk], third_r.at[chunk], back).start()

    for chunk in SEQUENCE[:AHEAD]:
        send(chunk)
    local = [
        pltpu.make_async_copy(eps.at[:, mine], e.at[pl.ds(1, planes)], eps_s.at[0]),
        pltpu.make_async_copy(eps.at[:, pl.ds(height - 8 * yh, 8)], eblock, eps_s.at[1]),
        pltpu.make_async_copy(orb.at[0, :, mine], o.at[0], own_s),
    ]
    for copy in local:
        copy.start()

    to_row = across, device(x + dx, 1 - yh, z, yl, core)
    first_plane, last_plane = dom == 0, dom == 4 * cz - 1
    has_after = jnp.where(yh == 0, 1.0, 0.0)
    has_before = 1.0 - has_after

    def plane_copies(gen, job, lower, upper, lower_to, upper_to):
        return [remote(lower, upper_to, plane_s.at[gen, job, 0], plane_r.at[gen, job, 0], to_plane[0]),
                remote(upper, lower_to, plane_s.at[gen, job, 1], plane_r.at[gen, job, 1], to_plane[1])]

    def halo_planes(gen, job):
        f = field.at[gen, job]
        return plane_copies(gen, job, f.at[1], f.at[planes], f.at[0], f.at[planes + 1])

    def halo_rows(gen, job):
        return [remote(pack.at[gen, job], rows.at[gen, job], row_s.at[gen, job], row_r.at[gen, job], to_row[job])]

    def start(copies):
        for copy in copies:
            copy.start()

    def finish_planes(gen, job):
        for side, edge, at in ((0, last_plane, planes + 1), (1, first_plane, 0)):
            arrived(field.at[gen, job, at], plane_r.at[gen, job, side])

            @pl.when(edge)
            def _():
                field[gen, job, at] = jnp.zeros((height, lanes), F32)

    local[0].wait()
    eps_planes = plane_copies(ITERS, 0, e.at[1], e.at[planes], e.at[0], e.at[planes + 1])
    start(eps_planes)
    local[1].wait()
    erows[0] = eblock[:, 7:8] * has_before
    erows[1] = eblock[:, 0:1] * has_after
    for side, edge, at in ((0, last_plane, planes + 1), (1, first_plane, 0)):
        arrived(e.at[at], plane_r.at[ITERS, 0, side])

        @pl.when(edge)
        def _():
            e[at] = jnp.zeros((height, lanes), F32)

    row_at = lax.broadcasted_iota(jnp.int32, (STRIP, lanes), 0)
    lane_at = lax.broadcasted_iota(jnp.int32, (STRIP, lanes), 1)

    def four(value, before, after):
        below = jnp.where(row_at == STRIP - 1, after, pltpu.roll(value, STRIP - 1, 0))
        above = jnp.where(row_at == 0, before, pltpu.roll(value, 1, 0))
        right = jnp.where(lane_at == lanes - 1, 0.0, pltpu.roll(value, lanes - 1, 1))
        left = jnp.where(lane_at == 0, 0.0, pltpu.roll(value, 1, 1))
        return below, above, right, left

    def weigh(p, carry):
        for r in range(0, height, STRIP):
            s = pl.ds(r, STRIP)
            value = e[p + 1, s]
            before = e[p + 1, r - 1 : r] if r else erows[0, p]
            after = e[p + 1, r + STRIP : r + STRIP + 1] if r + STRIP < height else erows[1, p]
            below, above, right, left = four(value, before, after)
            wyp[p, s] = (value + below) * (0.5 * SCALE)
            wym[p, s] = (value + above) * (0.5 * SCALE)
            wzp[p, s] = (value + right) * (0.5 * SCALE)
            wzm[p, s] = (value + left) * (0.5 * SCALE)
            wx[p, s] = (value + e[p, s]) * (0.5 * SCALE)
        return carry

    lax.fori_loop(0, planes, weigh, 0)
    wx[planes] = (e[planes] + e[planes + 1]) * (0.5 * SCALE)
    local[2].wait()

    def density(job, chunk):
        for i in range(step):
            p = chunk * step + i
            value = FOUR_PI * o[1, p] * o[2 * job, p]
            field[0, job, p + 1] = value
            pack[0, job, p] = value[height - 1 : height] * has_after + value[0:1] * has_before

    for n, chunk in enumerate(SEQUENCE):
        arrived(o.at[1, part(chunk)], far_r.at[chunk])
        if n + AHEAD < CHUNKS:
            send(SEQUENCE[n + AHEAD])
        density(0, chunk)
        if n == 1:
            start(halo_planes(0, 0))
        arrived(o.at[2, part(chunk)], third_r.at[chunk])
        density(1, chunk)
        if n == 1:
            start(halo_planes(0, 1))
    for job in range(2):
        start(halo_rows(0, job))

    def folded(value):
        total = value[0:8]
        for r in range(8, STRIP, 8):
            total = total + value[r : r + 8]
        return total[:, : lanes // 2] + total[:, lanes // 2 :]

    def apply(gen, job, strips, p, sums):
        first_sum, second_sum = sums
        for r in strips:
            s = pl.ds(r, STRIP)
            value = field[gen, job, p + 1, s]
            before = field[gen, job, p + 1, r - 1 : r] if r else rows[gen, job, p] * has_before
            last = r + STRIP == height
            after = rows[gen, job, p] * has_after if last else field[gen, job, p + 1, r + STRIP : r + STRIP + 1]
            below, above, right, left = four(value, before, after)
            result = wx[p + 1, s] * (value - field[gen, job, p + 2, s])
            result += wx[p, s] * (value - field[gen, job, p, s])
            result += wyp[p, s] * (value - below)
            result += wym[p, s] * (value - above)
            result += wzp[p, s] * (value - right)
            result += wzm[p, s] * (value - left)
            if gen < ITERS - 1:
                field[gen + 1, job, p + 1, s] = result
                if r == 0:
                    pack[gen + 1, job, p] = result[0:1] * has_before
                if last:
                    pack[gen + 1, job, p] += result[STRIP - 1 : STRIP] * has_after
            first_sum += folded(value * value)
            second_sum += folded(value * result)
        return first_sum, second_sum

    half_lanes = lanes // 2
    tile_row = lax.broadcasted_iota(jnp.int32, (16, half_lanes), 0)
    strips = list(range(0, height, STRIP))

    tile = jnp.zeros((16, half_lanes), F32)

    def power(gen, job, tile):
        sums = (jnp.zeros((8, half_lanes), F32),) * 2
        sums = lax.fori_loop(1, planes - 1, functools.partial(apply, gen, job, strips[1:-1]), sums)
        arrived(rows.at[gen, job], row_r.at[gen, job])
        sums = lax.fori_loop(1, planes - 1, functools.partial(apply, gen, job, (strips[0], strips[-1])), sums)
        finish_planes(gen, job)
        sums = lax.fori_loop(0, 2, lambda i, c: apply(gen, job, strips, i * (planes - 1), c), sums)
        if gen < ITERS - 1:
            start(halo_planes(gen + 1, job))
            start(halo_rows(gen + 1, job))
        for q in range(2):
            moment = jnp.sum(sums[q], axis=0, keepdims=True)
            tile = jnp.where(tile_row == 8 * job + 2 * gen + q, moment, tile)
        return tile

    for gen in range(ITERS):
        for job in range(2):
            tile = power(gen, job, tile)

    red[...] = tile
    for d in range(1, cz):
        remote(red, zin.at[d - 1], z_s.at[d - 1], z_r.at[d - 1], device(x, yh, z + d, yl, core)).start()
    for d in range(1, cz):
        arrived(zin.at[d - 1], z_r.at[d - 1])
        tile = tile + zin[d - 1]
    yred[...] = tile
    relations = [(x_, h, k, cc) for x_, h in ((0, 0), (0, 1), (1, 1)) for k in range(2) for cc in range(2)][1:]
    for at, (x_, h, k, cc) in enumerate(relations):
        remote(yred, yin.at[at], y_s.at[at], y_r.at[at],
               device(x + dx * x_, flip(yh, h), z, flip(yl, k), flip(core, cc))).start()
    for at, (x_, h, k, cc) in enumerate(relations):
        arrived(yin.at[at], y_r.at[at])
        other = yin[at]
        if h:
            other = jnp.where((tile_row // 8) == x_, other, 0.0)
        tile = tile + other

    total = jnp.broadcast_to(jnp.sum(tile, axis=1, keepdims=True), (16, half_lanes))
    coefficient = []
    for job in range(2):
        m = [jnp.broadcast_to(total[8 * job + k : 8 * job + k + 1], (8, half_lanes)) for k in range(6)]
        i1 = 1.0 / m[1]
        l1, l2 = m[2] * i1, m[3] * i1
        d2, f2 = m[3] - l1 * m[2], m[4] - l2 * m[2]
        i2 = 1.0 / d2
        l3 = f2 * i2
        d3 = m[5] - l2 * m[3] - l3 * f2
        g1 = m[1] - l1 * m[0]
        c2 = (m[2] - l2 * m[0] - l3 * g1) / d3
        c1 = g1 * i2 - l3 * c2
        c0 = m[0] * i1 - l1 * c1 - l2 * c2
        coefficient.append([jnp.concatenate([SCALE * c, SCALE * c], axis=1) for c in (c0, c1, c2)])

    def finish(chunk, carry):
        for i in range(step):
            p = chunk * step + i
            for r in range(0, height, 8):
                s = pl.ds(r, 8)
                potential = []
                for job in range(2):
                    value = coefficient[job][0] * field[0, job, p + 1, s]
                    for gen in range(1, ITERS):
                        value = value + coefficient[job][gen] * field[gen, job, p + 1, s]
                    potential.append(value)
                near, far, third = o[0, p, s], o[1, p, s], o[2, p, s]
                u_out[p, s] = -(potential[1] * far)
                far_out[p, s] = -(potential[0] * near + potential[1] * third)
                near_out[p, s] = -(potential[0] * far)
        remote(far_out.at[part(chunk)], out.at[0, part(chunk), mine], out_s.at[chunk], out_r.at[chunk], across).start()
        remote(u_out.at[part(chunk)], u_in.at[part(chunk)], u_s.at[chunk], u_r.at[chunk], aside).start()
        return carry

    lax.fori_loop(0, CHUNKS, finish, 0)

    def near_copy(chunk):
        return pltpu.make_async_copy(near_out.at[part(chunk)], out.at[0, part(chunk), mine], near_s.at[chunk])

    def finish_near(chunk, carry):
        arrived(u_in.at[part(chunk)], u_r.at[chunk])
        for i in range(step):
            p = chunk * step + i
            near_out[p] = near_out[p] + u_in[p]
        near_copy(chunk).start()
        return carry

    lax.fori_loop(0, CHUNKS, finish_near, 0)

    for chunk in range(CHUNKS):
        arrived(out.at[0, part(chunk), theirs], out_r.at[chunk])
        near_copy(chunk).wait()
        sent(far_out.at[part(chunk)], out_s.at[chunk])
        sent(u_out.at[part(chunk)], u_s.at[chunk])
        sent(orb.at[0, part(chunk), theirs], far_s.at[chunk])
        sent(orb.at[0, part(chunk), mine], third_s.at[chunk])
    for copy in eps_planes:
        copy.wait_send()
    for gen in range(ITERS):
        for job in range(2):
            for copy in halo_planes(gen, job) + halo_rows(gen, job):
                copy.wait_send()
    for d in range(cz - 1):
        sent(red, z_s.at[d])
    for at in range(11):
        sent(yred, y_s.at[at])


def per_device(cx, cz, orbitals, dielectric):
    _, deep, width, lanes = orbitals.shape
    planes, height = deep, width // 2
    full = (planes, height, lanes)
    vmem, dma = pltpu.VMEM, pltpu.SemaphoreType.DMA
    scratch = [
        vmem((3, *full), F32),
        vmem((planes + 2, height, lanes), F32),
        vmem((planes, 8, lanes), F32),
        vmem((planes + 1, height, lanes), F32),
        vmem(full, F32),
        vmem(full, F32),
        vmem(full, F32),
        vmem(full, F32),
        vmem((ITERS, 2, planes + 2, height, lanes), F32),
        vmem((ITERS, 2, planes, 1, lanes), F32),
        vmem((ITERS, 2, planes, 1, lanes), F32),
        vmem((2, planes, 1, lanes), F32),
        vmem((16, lanes // 2), F32),
        vmem((cz - 1, 16, lanes // 2), F32),
        vmem((16, lanes // 2), F32),
        vmem((11, 16, lanes // 2), F32),
        vmem(full, F32),
        vmem(full, F32),
        vmem(full, F32),
        vmem(full, F32),
        dma,
        *[dma((CHUNKS,))] * 4,
        dma((2,)),
        *[dma((ITERS + 1, 2, 2))] * 2,
        *[dma((ITERS, 2))] * 2,
        *[dma((cz - 1,))] * 2,
        *[dma((11,))] * 2,
        *[dma((CHUNKS,))] * 5,
    ]
    return pl.pallas_call(
        functools.partial(kernel, cx, cz),
        out_shape=jax.ShapeDtypeStruct(orbitals.shape, F32),
        in_specs=[pl.BlockSpec(memory_space=pl.ANY)] * 2,
        out_specs=pl.BlockSpec(memory_space=pl.ANY),
        scratch_shapes=scratch,
        compiler_params=pltpu.CompilerParams(
            collective_id=0, has_side_effects=True, vmem_limit_bytes=60 * 1024 * 1024
        ),
    )(orbitals, dielectric)


def solution(mesh):
    return jax.shard_map(
        functools.partial(per_device, mesh.shape["blk"] // 2, mesh.shape["dom"] // 4),
        mesh=mesh,
        in_specs=(P("blk", "dom", None, None), P("dom", None, None)),
        out_specs=P("blk", "dom", None, None),
        check_vma=False,
    )
```

profile of v0, /device:TPU:1, one launch (start us, length us, event | category | flops | bytes accessed | tf_op | source)
XLA Modules:
  0.0 100.5 jit_solution(5453226871577105720)
XLA Ops:
  0.0 97.5 %shard_map.28 = f32[1,8,256,256]{3,2,1,0:T(8,128)} custom-call(f32[1,8,256,256]{3,2,1,0:T(8,128)} %orb.1, f32[8,256,256]{2,1,0:T(8,128)} %eps.1), custom_call_target="tpu_custom_call" | custom-call | tf_op jit(solution)/shard_map/pallas_call | solution.py:354
  97.5 3.0 %copy.4 = f32[1,8,256,256]{3,2,1,0:T(8,128)} copy(f32[1,8,256,256]{3,2,1,0:T(8,128)} %shard_map.28) | data formatting | bytes 4194304
where the time goes:
time: 101 us
  Pallas kernels  97.5 us (97%)
  local copies, waits for them, and re-layouts  3.05 us (3%)
    pallas_call x1, Pallas kernels, per_device(): pl.pallas_call(functools.partial(kernel, cx, cz), out_shape=jax.ShapeDtyp...  97.5 us
    unnamed x1, local copies, waits for them, and re-layouts  3.05 us

commit v1 on v0

--- a/solution.py
+++ b/solution.py
@@ -159,6 +159,12 @@
             field[0, job, p + 1] = value
             pack[0, job, p] = value[height - 1 : height] * has_after + value[0:1] * has_before
 
+    def second_density(n, chunk):
+        arrived(o.at[2, part(chunk)], third_r.at[chunk])
+        density(1, chunk)
+        if n == 1:
+            start(halo_planes(0, 1))
+
     for n, chunk in enumerate(SEQUENCE):
         arrived(o.at[1, part(chunk)], far_r.at[chunk])
         if n + AHEAD < CHUNKS:
@@ -166,12 +172,10 @@
         density(0, chunk)
         if n == 1:
             start(halo_planes(0, 0))
-        arrived(o.at[2, part(chunk)], third_r.at[chunk])
-        density(1, chunk)
-        if n == 1:
-            start(halo_planes(0, 1))
-    for job in range(2):
-        start(halo_rows(0, job))
+        if n < CHUNKS - 1:
+            second_density(n, chunk)
+
+    start(halo_rows(0, 0))
 
     def folded(value):
         total = value[0:8]
@@ -213,6 +217,9 @@
     def power(gen, job, tile):
         sums = (jnp.zeros((8, half_lanes), F32),) * 2
         sums = lax.fori_loop(1, planes - 1, functools.partial(apply, gen, job, strips[1:-1]), sums)
+        if gen == job == 0:
+            second_density(CHUNKS - 1, SEQUENCE[-1])
+            start(halo_rows(0, 1))
         arrived(rows.at[gen, job], row_r.at[gen, job])
         sums = lax.fori_loop(1, planes - 1, functools.partial(apply, gen, job, (strips[0], strips[-1])), sums)
         finish_planes(gen, job)
@@ -230,14 +237,14 @@
             tile = power(gen, job, tile)
 
     red[...] = tile
-    for d in range(1, cz):
+    for d in sorted(range(1, cz), key=lambda d: -min(d, cz - d)):
         remote(red, zin.at[d - 1], z_s.at[d - 1], z_r.at[d - 1], device(x, yh, z + d, yl, core)).start()
     for d in range(1, cz):
         arrived(zin.at[d - 1], z_r.at[d - 1])
         tile = tile + zin[d - 1]
     yred[...] = tile
     relations = [(x_, h, k, cc) for x_, h in ((0, 0), (0, 1), (1, 1)) for k in range(2) for cc in range(2)][1:]
-    for at, (x_, h, k, cc) in enumerate(relations):
+    for at, (x_, h, k, cc) in reversed(list(enumerate(relations))):
         remote(yred, yin.at[at], y_s.at[at], y_r.at[at],
                device(x + dx * x_, flip(yh, h), z, flip(yl, k), flip(core, cc))).start()
     for at, (x_, h, k, cc) in enumerate(relations):

time: 101 us -> 99.9 us (0.989)
  no operation moved by 1% of the time
where the time goes in v1:
time: 99.9 us; the launch traced here: 99.8 us
  Pallas kernels  96.8 us (97%)
  local copies, waits for them, and re-layouts  3.05 us (3%)
    pallas_call x1, Pallas kernels, per_device(): pl.pallas_call(functools.partial(kernel, cx, cz), out_shape=jax.ShapeDtyp...  96.8 us
    unnamed x1, local copies, waits for them, and re-layouts  3.05 us

profile of v1, /device:TPU:1, one launch (start us, length us, event | category | flops | bytes accessed | tf_op | source)
XLA Modules:
  0.0 99.8 jit_solution(1165943109973550884)
XLA Ops:
  0.0 96.8 %shard_map.28 = f32[1,8,256,256]{3,2,1,0:T(8,128)} custom-call(f32[1,8,256,256]{3,2,1,0:T(8,128)} %orb.1, f32[8,256,256]{2,1,0:T(8,128)} %eps.1), custom_call_target="tpu_custom_call" | custom-call | tf_op jit(solution)/shard_map/pallas_call | solution.py:361
  96.8 3.0 %copy.4 = f32[1,8,256,256]{3,2,1,0:T(8,128)} copy(f32[1,8,256,256]{3,2,1,0:T(8,128)} %shard_map.28) | data formatting | bytes 4194304
